TPU v7x, 128 devices: a whole 4x4x4 slice. The times are simulated.
128 devices in a mesh: pair: 32 (over x, y, core), orb: 4 (over z).
Axes of the slice: x: 4, y: 4, z: 4, core: 2. Of those that a mesh axis runs over, the one named last changes fastest.
Arguments:
- integral_tiles: bfloat16 [1536, 40, 128, 128], P(('pair', 'orb')), may hold values from -6 to 6
- tile_lam: int32 [1536], P(('pair', 'orb')), may hold values from 0 to 95
- tile_sig: int32 [1536], P(('pair', 'orb')), may hold values from 0 to 2
- tile_rows: int32 [1536], P(('pair', 'orb')), may hold values from 1 to 40
- screen_mask: int32 [1536], P(('pair', 'orb')), may hold values 0 or 1
- occ_panel: bfloat16 [64, 12288], P(None, ('pair', 'orb')), may hold values from -0.5 to 0.5
- virt_panel: bfloat16 [12288, 11264], P('pair', 'orb'), may hold values from -0.0546875 to 0.0546875
Outputs:
- transformed: bfloat16 [64, 40, 11264], P('pair', None, 'orb')
All inputs are finite; a program needn't handle non-finite values. No bound on the sum of `screen_mask` on one device may be relied on, other than what follows from the above.
Results may differ from a plain program's by a relative error of at most 0.033.
Values may be sent and summed in bfloat16 or wider, within the bound.
A program may use at most 128 MiB of HBM per device.

v0:
```python
import jax
import jax.numpy as jnp
from jax import lax
from jax.sharding import PartitionSpec as P

BS = 128
NOCC = 64


def body(integral_tiles, tile_lam, tile_sig, tile_rows, screen_mask, occ_panel, virt_panel):
    occ_full = lax.all_gather(occ_panel, ("pair", "orb"), axis=1, tiled=True)
    slot_total = integral_tiles.shape[0]
    row_total = integral_tiles.shape[1]
    sig_width = virt_panel.shape[0]
    owned_blocks = sig_width // BS
    occ_blocks = occ_full.reshape(NOCC, occ_full.shape[1] // BS, BS)
    picked = jnp.take(occ_blocks, tile_lam, axis=1)
    half_terms = jnp.einsum(
        "jtl,trls->tjrs", picked, integral_tiles, preferred_element_type=jnp.float32
    )
    row_ids = lax.broadcasted_iota(jnp.int32, (slot_total, row_total), 1)
    row_live = ((row_ids < tile_rows[:, None]) & (screen_mask[:, None] > 0)).astype(jnp.float32)
    block_ids = lax.broadcasted_iota(jnp.int32, (slot_total, owned_blocks), 1)
    onehot = (block_ids == tile_sig[:, None]).astype(jnp.float32)
    partial_value = jnp.einsum(
        "tb,tr,tjrs->jrbs", onehot, row_live, half_terms, precision=lax.Precision.HIGHEST
    )
    partial_value = partial_value.reshape(NOCC, row_total, sig_width)
    occ_half = lax.psum(partial_value.astype(jnp.bfloat16), "orb")
    virt_width = virt_panel.shape[1]
    owned_rows = NOCC // lax.axis_size("pair")
    flat_rows = occ_half.reshape(lax.axis_size("pair") * owned_rows * row_total, sig_width)
    product = jnp.dot(flat_rows, virt_panel, preferred_element_type=jnp.float32)
    return lax.psum_scatter(
        product.reshape(lax.axis_size("pair") * owned_rows, row_total, virt_width).astype(
            jnp.bfloat16
        ),
        "pair",
        scatter_dimension=0,
        tiled=True,
    )


def solution(mesh):
    return jax.shard_map(
        body,
        mesh=mesh,
        in_specs=(
            P(("pair", "orb"), None, None, None),
            P(("pair", "orb")),
            P(("pair", "orb")),
            P(("pair", "orb")),
            P(("pair", "orb")),
            P(None, ("pair", "orb")),
            P("pair", "orb"),
        ),
        out_specs=P("pair", None, "orb"),
        check_vma=False,
    )
```

profile of v0, /device:TPU:1, one launch (start us, length us, event | category | flops | bytes accessed | tf_op | source)
XLA Modules:
  0.0 319.3 jit_solution(5792794216264188940)
XLA Ops:
  6.5 0.0 copy-start
  6.5 0.0 all-gather.3.cloned.1.call-start
  6.5 0.7 all-gather.3.cloned.1.call-update
  7.3 0.0 all-reduce.2.cloned.1.call-start
  7.3 0.7 compare_select_fusion
  8.0 0.7 compare_and_fusion
  8.6 0.7 broadcast_compare_fusion
  9.3 0.7 fusion.10
  10.0 69.3 %all-gather.3.cloned.1.call-done = bf16[128,96,64]{1,2,0:T(8,128)(2,1)} async-done(((bf16[1,96,64]{1,2,0:T(8,128)(2,1)}), bf16[128,96,64]{1,2,0:T(8,128)(2,1)}) %all-gather.3.cloned.1.call-update) | async-done | bytes 1572880 | tf_op jit(solution)/shard_map/all_gather | solution.py:11
  79.3 4.3 %copy.12 = bf16[128,96,64]{1,0,2:T(8,128)(2,1)} copy(bf16[128,96,64]{1,2,0:T(8,128)(2,1)} %all-gather.3.cloned.1.call-done) | data formatting | bytes 3145728 | tf_op jit(solution)/shard_map/all_gather | solution.py:11
  83.6 5.0 %reshape.29 = bf16[12288,64]{0,1:T(8,128)(2,1)} reshape(bf16[128,96,64]{1,0,2:T(8,128)(2,1)} %copy.12) | data formatting | bytes 3145728
  88.6 3.0 copy_bitcast_fusion
  91.6 2.0 gather_fusion
  93.6 0.0 copy-start.1
  93.6 6.8 %broadcast_multiply_fusion = f32[12,64,40,128]{3,1,2,0:T(8,128)S(1)} fusion(f32[12,40]{1,0:T(8,128)S(1)} %fusion.10, bf16[12,40,128,128]{3,2,1,0:T(8,128)(2,1)} %param.7, bf16[12,64,128]{2,1,0:T(8,128)(2,1)S(1)} %gather_fusion, pred[12]{0:T(512)(128)(4,1)S(1)} %compare_and_fusion), kind=kOutput, calls=%fused_computation.4 | convolution fusion | flops 1010663424 | bytes 31655820 | tf_op jit(solution)/shard_map/jtl,trls->tjrs/dot_general | solution.py:18
  100.3 0.0 copy-done.1
  100.4 31.4 %convert_bitcast_fusion = bf16[64,40,3,128]{3,2,1,0:T(4,128)(2,1)} fusion(f32[12,64,40,128]{3,1,2,0:T(8,128)S(1)} %broadcast_multiply_fusion, s32[12]{0:T(128)S(1)} %copy-done.1), kind=kOutput, calls=%fused_computation.5 | convolution fusion | flops 142540832 | bytes 17694768 | tf_op jit(solution)/shard_map/tb,tr,tjrs->jrbs/dot_general | solution.py:25
  131.7 6.1 %convert_element_type.16 = bf16[64,40,384]{2,1,0:T(8,128)(2,1)} reshape(bf16[64,40,3,128]{3,2,1,0:T(4,128)(2,1)} %convert_bitcast_fusion) | data formatting | bytes 3932160 | tf_op jit(solution)/shard_map/convert_element_type | solution.py:29
  137.8 0.0 all-reduce.2.cloned.1.call-update
  137.9 0.0 reduce-scatter.2.cloned.1.call-start
  137.9 54.0 %all-reduce.2.cloned.1.call-done = bf16[64,40,384]{2,1,0:T(8,128)(2,1)} async-done(((bf16[64,40,384]{2,1,0:T(8,128)(2,1)}), bf16[64,40,384]{2,1,0:T(8,128)(2,1)}) %all-reduce.2.cloned.1.call-update) | async-done | bytes 1966096 | tf_op jit(solution)/shard_map/psum | solution.py:29
  191.9 0.0 copy-done
  191.9 13.1 %convolution_convert_fusion = bf16[64,40,2816]{2,1,0:T(8,128)(2,1)} fusion(bf16[64,40,384]{2,1,0:T(8,128)(2,1)} %all-reduce.2.cloned.1.call-done, bf16[384,2816]{1,0:T(8,128)(2,1)S(1)} %copy-done), kind=kOutput, calls=%fused_computation.3 | convolution fusion | flops 5543690240 | bytes 18546688 | tf_op jit(solution)/shard_map/dot_general | solution.py:33
  204.9 0.0 reduce-scatter.2.cloned.1.call-update
  205.0 107.8 %reduce-scatter.2.cloned.1.call-done = bf16[2,40,2816]{2,1,0:T(8,128)(2,1)} async-done(((bf16[64,40,2816]{2,1,0:T(8,128)(2,1)}), bf16[2,40,2816]{2,1,0:T(8,128)(2,1)}) %reduce-scatter.2.cloned.1.call-update) | async-done | bytes 450576 | tf_op jit(solution)/shard_map/reduce_scatter | solution.py:34
  (1 shorter events, 0.0 us)
Async XLA Ops:
  6.5 185.3 %copy-start = (bf16[384,2816]{1,0:T(8,128)(2,1)S(1)}, bf16[384,2816]{1,0:T(8,128)(2,1)}, u32[]{:S(2)}) copy-start(bf16[384,2816]{1,0:T(8,128)(2,1)} %param.13) | copy-start | bytes 6488068
  6.5 72.8 %all-gather.3.cloned.1.call-start = ((), (), s32[]{:S(2)}) async-start(), calls=%async_computation.3 | async-start | bytes 2113536 | tf_op jit(solution)/shard_map/all_gather | solution.py:11
  7.3 184.6 %all-reduce.2.cloned.1.call-start = ((), (), s32[]{:S(2)}) async-start(), calls=%async_computation.1 | async-start | bytes 3932160 | tf_op jit(solution)/shard_map/psum | solution.py:29
  93.6 6.8 %copy-start.1 = (s32[12]{0:T(128)S(1)}, s32[12]{0:T(128)}, u32[]{:S(2)}) copy-start(s32[12]{0:T(128)} %param.9) | copy-start | bytes 148
  137.9 174.9 %reduce-scatter.2.cloned.1.call-start = ((), (), s32[]{:S(2)}) async-start(), calls=%async_computation.2 | async-start | bytes 14868480 | tf_op jit(solution)/shard_map/reduce_scatter | solution.py:34
Sparse Core Ops, SparseCore 0:
  10.4 68.8 all-gather.2
  138.0 53.8 all-reduce.1
  205.1 107.6 reduce-scatter.1
where the time goes:
time: 320 us; the launch traced here: 319 us
  waiting for transfers between devices  232 us (72%)
  matrix products  51.2 us (16%)
  local copies, waits for them, and re-layouts  20.4 us (6%)
  between operations  13.1 us (4%)
    reduce_scatter x1, waiting for transfers between devices, body(): lax.psum_scatter(product.reshape(lax.axis_size('pair') * owned_rows, row_...  108 us
    all_gather x1, waiting for transfers between devices, body(): occ_full = lax.all_gather(occ_panel, ('pair', 'orb'), axis=1, tiled=True)  69.3 us
    psum x1, waiting for transfers between devices, body(): occ_half = lax.psum(partial_value.astype(jnp.bfloat16), 'orb')  54 us
    dot_general x1, matrix products, body(): jnp.einsum('tb,tr,tjrs->jrbs', onehot, row_live, half_terms, precision=la...  31.4 us
    dot_general x1, matrix products, body(): product = jnp.dot(flat_rows, virt_panel, preferred_element_type=jnp.float32)  13.1 us
    dot_general x1, matrix products, body(): jnp.einsum('jtl,trls->tjrs', picked, integral_tiles, preferred_element_ty...  6.76 us
  transfers between devices with their start and end apart: 3, of which 3 were waited for; matrix products, arithmetic and copies ran while one was open for 1% of the time, Pallas kernels for 0%

commit v1 on v0

v1 whole, which is shorter than its diff:
```python
import jax
import jax.numpy as jnp
from jax import lax
from jax.experimental import pallas as pl
from jax.experimental.pallas import tpu as pltpu
from jax.sharding import PartitionSpec as P

BS = 128
NOCC = 64
ROWS = 40
SLOTS = 12
NBLK = 96
SIG = 3
KW = 384
NW = 2816
HW = NW // 2
CUT = 768
BR = 80
MESH = pl.DeviceIdType.MESH
F32 = jnp.float32
BF16 = jnp.bfloat16


def place():
    pair = lax.axis_index("pair")
    return pair, pair // 8, (pair // 2) % 4, pair % 2, lax.axis_index("orb")


def pair_of(x, y, c):
    return (x * 4 + y) * 2 + c


def push(src, dst, send_sem, recv_sem, pair, z):
    return pltpu.make_async_remote_copy(
        src_ref=src,
        dst_ref=dst,
        send_sem=send_sem,
        recv_sem=recv_sem,
        device_id=(pair, z),
        device_id_type=MESH,
    )


def gather_kernel(occ_ref, out_ref, zbuf, gat, zs, zr, ss, sr, cs, cr, out_sem):
    pair, x, y, c, z = place()
    barrier = pltpu.get_barrier_semaphore()

    def hello(pair_id, z_id):
        pl.semaphore_signal(barrier, inc=1, device_id=(pair_id, z_id), device_id_type=MESH)

    hello(pair_of(x, y, 1 - c), z)
    for d in range(1, 4):
        hello(pair_of((x + d) % 4, y, c), z)
        hello(pair_of(x, (y + d) % 4, c), z)
        hello(pair, (z + d) % 4)
    zbuf[z] = jnp.concatenate([occ_ref[...], jnp.zeros((NOCC, 32), BF16)], axis=1)
    pl.semaphore_wait(barrier, 10)

    sends = []

    def start(copy):
        copy.start()
        sends.append(copy)
        return copy

    steps = [
        start(push(zbuf.at[z], zbuf.at[z], zs.at[d - 1], zr.at[d - 1], pair, (z + d) % 4))
        for d in range(1, 4)
    ]
    for copy in steps:
        copy.wait_recv()
    whole = jnp.concatenate([zbuf[i][:, :96] for i in range(4)], axis=1)
    for k in range(3):
        gat[x, y, c, k] = whole[:, k * BS : (k + 1) * BS]

    lo, hi = pl.ds(0, 32), pl.ds(32, 32)
    first_a, first_b = [], []
    for d in range(1, 4):
        view = gat.at[x, y, c, :, lo]
        first_a.append(
            start(push(view, view, ss.at[0, d - 1], sr.at[0, d - 1], pair_of((x + d) % 4, y, c), z))
        )
        view = gat.at[x, y, c, :, hi]
        first_b.append(
            start(push(view, view, ss.at[1, d - 1], sr.at[1, d - 1], pair_of(x, (y + d) % 4, c), z))
        )
    other = pair_of(x, y, 1 - c)
    for copy in first_a:
        copy.wait_recv()
    second_a, second_b, across = [], [], []
    row = gat.at[:, y, c, :, lo]
    for d in range(1, 4):
        second_a.append(
            start(push(row, row, ss.at[2, d - 1], sr.at[2, d - 1], pair_of(x, (y + d) % 4, c), z))
        )
    across.append(start(push(row, row, cs.at[0, 0], cr.at[0, 0], other, z)))
    for copy in first_b:
        copy.wait_recv()
    col = gat.at[x, :, c, :, hi]
    for d in range(1, 4):
        second_b.append(
            start(push(col, col, ss.at[3, d - 1], sr.at[3, d - 1], pair_of((x + d) % 4, y, c), z))
        )
    across.append(start(push(col, col, cs.at[1, 0], cr.at[1, 0], other, z)))
    for d in range(1, 4):
        second_a[d - 1].wait_recv()
        row = gat.at[:, (y - d + 4) % 4, c, :, lo]
        across.append(start(push(row, row, cs.at[0, d], cr.at[0, d], other, z)))
        second_b[d - 1].wait_recv()
        col = gat.at[(x - d + 4) % 4, :, c, :, hi]
        across.append(start(push(col, col, cs.at[1, d], cr.at[1, d], other, z)))
    for copy in across:
        copy.wait_recv()
    done = pltpu.make_async_copy(gat, out_ref, out_sem)
    done.start()
    for copy in sends:
        copy.wait_send()
    done.wait()


def gather_panel(occ_panel):
    sem = pltpu.SemaphoreType.DMA
    return pl.pallas_call(
        gather_kernel,
        out_shape=jax.ShapeDtypeStruct((4, 4, 2, 3, NOCC, BS), BF16),
        in_specs=[pl.BlockSpec(memory_space=pltpu.VMEM)],
        out_specs=pl.BlockSpec(memory_space=pl.ANY),
        scratch_shapes=[
            pltpu.VMEM((4, NOCC, BS), BF16),
            pltpu.VMEM((4, 4, 2, 3, NOCC, BS), BF16),
            sem((3,)),
            sem((3,)),
            sem((4, 3)),
            sem((4, 3)),
            sem((2, 4)),
            sem((2, 4)),
            sem,
        ],
        compiler_params=pltpu.CompilerParams(
            collective_id=0, has_side_effects=True, vmem_limit_bytes=16 * 2**20
        ),
        name="gather_panel",
    )(occ_panel)


def tiles_kernel(lam, sig, rows, mask, tile_ref, occ_ref, out_ref, lhs, acc):
    step = pl.program_id(0)

    @pl.when(step == 0)
    def _():
        lhs[...] = jnp.zeros_like(lhs)
        for t in range(SLOTS):

            @pl.when(mask[t] > 0)
            def _():
                at = pl.multiple_of(sig[t] * NOCC, NOCC)
                lhs[pl.ds(at, NOCC), t * BS : (t + 1) * BS] = occ_ref[lam[t]]

    left = lhs[...]
    for q in range(4):
        parts = []
        for t in range(SLOTS):
            both = []
            for i in range(2):
                live = step * 8 + 2 * q + i < rows[t]
                tile = tile_ref[t, 2 * q + i]
                both.append(jnp.where(live, tile, jnp.zeros_like(tile)))
            parts.append(jnp.concatenate(both, axis=1))
        got = jnp.dot(left, jnp.concatenate(parts, axis=0), preferred_element_type=F32)
        for i in range(2):
            for s in range(SIG):
                acc[s, pl.ds(step * 8 + 2 * q + i, NOCC, stride=ROWS), :] = got[
                    s * NOCC : (s + 1) * NOCC, i * BS : (i + 1) * BS
                ]

    @pl.when(step == pl.num_programs(0) - 1)
    def _():
        @pl.loop(0, NOCC * ROWS, step=64)
        def _(r):
            r = pl.multiple_of(r, 64)
            for s in range(SIG):
                out_ref[pl.ds(r, 64), s * BS : (s + 1) * BS] = acc[s, pl.ds(r, 64), :].astype(BF16)


def tile_sums(lam, sig, rows, mask, tiles, occ):
    return pl.pallas_call(
        tiles_kernel,
        grid_spec=pltpu.PrefetchScalarGridSpec(
            num_scalar_prefetch=4,
            grid=(ROWS // 8,),
            in_specs=[
                pl.BlockSpec((SLOTS, 8, BS, BS), lambda i, *_: (0, i, 0, 0)),
                pl.BlockSpec((NBLK, NOCC, BS), lambda i, *_: (0, 0, 0)),
            ],
            out_specs=pl.BlockSpec((NOCC * ROWS, KW), lambda i, *_: (0, 0)),
            scratch_shapes=[
                pltpu.VMEM((SIG * NOCC, SLOTS * BS), BF16),
                pltpu.VMEM((SIG, NOCC * ROWS, BS), F32),
            ],
        ),
        out_shape=jax.ShapeDtypeStruct((NOCC * ROWS, KW), BF16),
        compiler_params=pltpu.CompilerParams(vmem_limit_bytes=48 * 2**20),
        name="tile_sums",
    )(lam, sig, rows, mask, tiles, occ)


CHUNKS = [
    [(2, 2), (2, 1), (2, 3), (2, 0)],
    [(1, 2), (3, 2), (1, 0), (3, 0)],
    [(1, 1), (1, 3), (3, 1), (3, 3)],
    [(0, 2), (0, 1), (0, 3), (0, 0)],
]
AT = {block: (k, i) for k, chunk in enumerate(CHUNKS) for i, block in enumerate(chunk)}
UP = (2, 1)


def transform_kernel(
    a_ref, b_ref, out_ref, b2, zin, red, a2, cc, ra, rb, rc, rd, re, rf, rg, rh,
    b_sem, zss, zrs, ags, agr, as_, ar, bs_, br, cs_, cr, ds_, dr, es_, er, fs_, fr, gs_, gr, hs_, hr,
):
    pair, x, y, c, z = place()
    barrier = pltpu.get_barrier_semaphore()
    xs = {1: pair_of((x + 1) % 4, y, c), -1: pair_of((x + 3) % 4, y, c)}
    ys = {1: pair_of(x, (y + 1) % 4, c), -1: pair_of(x, (y + 3) % 4, c)}

    def hello(pair_id, z_id):
        pl.semaphore_signal(barrier, inc=1, device_id=(pair_id, z_id), device_id_type=MESH)

    for d in range(4):
        if d:
            hello(pair, (z + d) % 4)
        hello(pair_of(x, y, 1 - c), (z + d) % 4)
    for d in (1, -1):
        hello(xs[d], z)
        hello(ys[d], z)
    pl.semaphore_wait(barrier, 11)

    own_k = pl.ds(pl.multiple_of(c * KW, BS), KW)
    other_k = pl.ds(pl.multiple_of((1 - c) * KW, BS), KW)
    b_own = pltpu.make_async_copy(b_ref, b2.at[own_k], b_sem.at[0])
    b_own.start()
    b_away = push(b_ref, b2.at[own_k], b_sem.at[1], b_sem.at[2], pair_of(x, y, 1 - c), z)
    b_away.start()
    sends = [b_away]

    def start(copy):
        copy.start()
        sends.append(copy)

    def z_copies(k):
        for zt in range(4):
            dx, dy = CHUNKS[k][zt]
            block = ((x + dx) % 4) * 4 + (y + dy) % 4
            yield zt, block, push(a_ref.at[block], zin.at[k, z], zss.at[k, zt], zrs.at[k, z], pair, zt)

    def z_send(k):
        for zt, block, copy in z_copies(k):

            @pl.when(z != zt)
            def _():
                copy.start()

            @pl.when(z == zt)
            def _():
                zin[k, zt] = a_ref[block]

    def z_reduce(k):
        for zf in range(4):

            @pl.when(z != zf)
            def _():
                push(zin.at[k, zf], zin.at[k, zf], zss.at[k, zf], zrs.at[k, zf], pair, zf).wait_recv()

        for core in range(2):
            for r in range(0, BR, 16):
                total = zin[k, 0, core, r : r + 16].astype(F32)
                for zf in range(1, 4):
                    total = total + zin[k, zf, core, r : r + 16].astype(F32)
                red[k, core, r : r + 16] = total.astype(BF16)

    def spread_copies(k):
        for core in range(2):
            for zt in range(4):
                remote = jnp.logical_or(c != core, z != zt)
                yield remote, push(
                    red.at[k, core], a2.at[k, c, z], ags.at[k, core, zt], agr.at[k, c, z],
                    pair_of(x, y, core), zt,
                )

    def spread(k):
        for remote, copy in spread_copies(k):

            @pl.when(remote)
            def _():
                copy.start()

        a2[k, c, z] = red[k, c]

    def spread_wait(k):
        for core in range(2):
            for zf in range(4):

                @pl.when(jnp.logical_or(c != core, z != zf))
                def _():
                    push(
                        red.at[k, core], a2.at[k, core, zf], ags.at[k, core, zf], agr.at[k, core, zf],
                        pair_of(x, y, core), zf,
                    ).wait_recv()

    def multiply(k):
        left = jnp.concatenate([a2[k, i].reshape(4 * BR, KW) for i in range(2)], axis=1)

        def tile(h, at, width):
            got = jnp.dot(left, b2[:, pl.ds(h * HW + at, width)], preferred_element_type=F32)
            cc[k, h, :, :, pl.ds(at, width)] = got.astype(BF16).reshape(4, BR, width)

        for h in range(2):

            @pl.loop(0, HW // 256)
            def _(j):
                tile(h, pl.multiple_of(j * 256, 256), 256)

            tile(h, HW - BS, BS)

    def held(h, block):
        k, i = AT[block]
        return cc.at[k, h, i]

    def add(into, terms, lo=0, hi=HW, out=None):
        for r in range(0, BR, 16):
            total = into[r : r + 16, lo:hi].astype(F32)
            for term in terms:
                total = total + term[r : r + 16, lo:hi].astype(F32)
            if out is None:
                into[r : r + 16, lo:hi] = total.astype(BF16)
            else:
                out_ref[r : r + 16, out : out + hi - lo] = total.astype(BF16)

    halves = {1: pl.ds(0, CUT), -1: pl.ds(CUT, HW - CUT)}

    def halves_out(src, dst, send_sem, recv_sem, to):
        for i, d in enumerate((1, -1)):
            start(push(src.at[:, halves[d]], dst.at[:, halves[d]], send_sem.at[i], recv_sem.at[i], to[d], z))

    def half_add(into, dst, send_sem, recv_sem, d, to):
        i = 0 if d == 1 else 1
        push(dst.at[:, halves[d]], dst.at[:, halves[d]], send_sem.at[i], recv_sem.at[i], to[d], z).wait_recv()
        add(into, [dst], 0 if d == 1 else CUT, CUT if d == 1 else HW)

    def arrived(dst, send_sem, recv_sem):
        push(dst, dst, send_sem, recv_sem, pair_of(x, y, 1 - c), z).wait_recv()

    def x_far():
        for dy in (2, 1, 3, 0):
            d = 1 if dy in UP else -1
            start(push(held(0, (2, dy)), ra.at[dy], as_.at[dy], ar.at[dy], xs[d], z))

    def x_near(blocks):
        order = sorted(blocks, key=lambda b: (b[1] in UP) == (b[0] == 1))
        for dx, dy in order:
            d = 1 if dx == 1 else -1
            if (dy in UP) == (dx == 1):
                arrived(ra.at[dy], as_.at[dy], ar.at[dy])
                add(held(0, (dx, dy)), [ra.at[dy]])
            i = 0 if d == 1 else 1
            start(push(held(0, (dx, dy)), rb.at[i, dy], bs_.at[i, dy], br.at[i, dy], xs[d], z))

    def x_home(dy):
        for i in range(2):
            arrived(rb.at[i, dy], bs_.at[i, dy], br.at[i, dy])
        add(held(0, (0, dy)), [rb.at[0, dy], rb.at[1, dy]])

    def near(h, block, far, far_s, far_r, dst, send_sem, recv_sem, d, to):
        half_add(held(h, block), far, far_s, far_r, d, to)
        i = 0 if d == 1 else 1
        start(push(held(h, block), dst.at[i], send_sem.at[i], recv_sem.at[i], to[d], z))

    def y_far(dx):
        halves_out(held(1, (dx, 2)), re.at[dx], es_.at[dx], er.at[dx], ys)

    def y_near(dx):
        for d in (1, -1):
            near(1, (dx, d % 4), re.at[dx], es_.at[dx], er.at[dx], rf.at[dx], fs_.at[dx], fr.at[dx], d, ys)

    def y_home(dx):
        for i in range(2):
            arrived(rf.at[dx, i], fs_.at[dx, i], fr.at[dx, i])
        add(held(1, (dx, 0)), [rf.at[dx, 0], rf.at[dx, 1]])

    z_send(0)
    z_send(1)
    z_reduce(0)
    spread(0)
    z_send(2)
    z_reduce(1)
    spread(1)
    z_send(3)
    b_own.wait()
    push(b_ref, b2.at[other_k], b_sem.at[1], b_sem.at[2], pair_of(x, y, 1 - c), z).wait_recv()
    spread_wait(0)
    multiply(0)
    y_far(2)
    x_far()
    z_reduce(2)
    spread(2)
    y_near(2)
    spread_wait(1)
    multiply(1)
    y_far(1)
    y_far(3)
    x_near(CHUNKS[1])
    z_reduce(3)
    spread(3)
    spread_wait(2)
    multiply(2)
    y_near(1)
    y_near(3)
    x_near(CHUNKS[2])
    y_home(2)
    halves_out(held(1, (2, 0)), rg, gs_, gr, xs)
    spread_wait(3)
    multiply(3)
    y_far(0)
    x_home(2)
    halves_out(held(0, (0, 2)), rc, cs_, cr, ys)
    y_home(1)
    near(1, (1, 0), rg, gs_, gr, rh, hs_, hr, 1, xs)
    y_home(3)
    near(1, (3, 0), rg, gs_, gr, rh, hs_, hr, -1, xs)
    y_near(0)
    x_home(1)
    near(0, (0, 1), rc, cs_, cr, rd, ds_, dr, 1, ys)
    x_home(3)
    near(0, (0, 3), rc, cs_, cr, rd, ds_, dr, -1, ys)
    x_home(0)
    y_home(0)
    for i in range(2):
        arrived(rh.at[i], hs_.at[i], hr.at[i])
    add(held(1, (0, 0)), [rh.at[0], rh.at[1]], out=HW)
    for i in range(2):
        arrived(rd.at[i], ds_.at[i], dr.at[i])
    add(held(0, (0, 0)), [rd.at[0], rd.at[1]], out=0)

    for copy in sends:
        copy.wait_send()
    for k in range(4):
        for zt, _, copy in z_copies(k):

            @pl.when(z != zt)
            def _():
                copy.wait_send()

        for remote, copy in spread_copies(k):

            @pl.when(remote)
            def _():
                copy.wait_send()


def transform(a, b):
    sem = pltpu.SemaphoreType.DMA

    def vm(*shape):
        return pltpu.VMEM(shape, BF16)

    pairs = [(4,), (2, 4), (2,), (2,), (4, 2), (4, 2), (2,), (2,)]
    return pl.pallas_call(
        transform_kernel,
        out_shape=jax.ShapeDtypeStruct((BR, NW), BF16),
        in_specs=[pl.BlockSpec(memory_space=pltpu.VMEM), pl.BlockSpec(memory_space=pl.ANY)],
        out_specs=pl.BlockSpec(memory_space=pltpu.VMEM),
        scratch_shapes=[
            vm(2 * KW, NW),
            vm(4, 4, 2, BR, KW),
            vm(4, 2, BR, KW),
            vm(4, 2, 4, BR, KW),
            vm(4, 2, 4, BR, HW),
            vm(4, BR, HW),
            vm(2, 4, BR, HW),
            vm(BR, HW),
            vm(2, BR, HW),
            vm(4, BR, HW),
            vm(4, 2, BR, HW),
            vm(BR, HW),
            vm(2, BR, HW),
            sem((3,)),
            sem((4, 4)),
            sem((4, 4)),
            sem((4, 2, 4)),
            sem((4, 2, 4)),
            *[sem(shape) for shape in pairs for _ in range(2)],
        ],
        compiler_params=pltpu.CompilerParams(
            collective_id=1, has_side_effects=True, vmem_limit_bytes=56 * 2**20
        ),
        name="transform",
    )(a, b)


def body(integral_tiles, tile_lam, tile_sig, tile_rows, screen_mask, occ_panel, virt_panel):
    occ = gather_panel(occ_panel).reshape(NBLK, NOCC, BS)
    sums = tile_sums(tile_lam, tile_sig, tile_rows, screen_mask, integral_tiles, occ)
    out = transform(sums.reshape(16, 2, BR, KW), virt_panel)
    return out.reshape(2, ROWS, NW)


def solution(mesh):
    return jax.shard_map(
        body,
        mesh=mesh,
        in_specs=(
            P(("pair", "orb"), None, None, None),
            P(("pair", "orb")),
            P(("pair", "orb")),
            P(("pair", "orb")),
            P(("pair", "orb")),
            P(None, ("pair", "orb")),
            P("pair", "orb"),
        ),
        out_specs=P("pair", None, "orb"),
        check_vma=False,
    )
```

time: 320 us -> 114 us (0.36)
  waiting for transfers between devices: 232 us -> 0 us
  Pallas kernels: 0 us -> 107 us
  matrix products: 51.2 us -> 0 us
  local copies, waits for them, and re-layouts: 20.4 us -> 6.44 us
  between operations: 13.1 us -> 0.05 us
    reduce_scatter x1 -> x0, waiting for transfers between devices: 108 us -> none  [body(): lax.psum_scatter(product.reshape(lax.axis_size('pair') * owned_rows, row_...]
    pallas_call x0 -> x3, Pallas kernels: none -> 107 us  [the longest x1 74.8 us: transform(): pl.pallas_call(transform_kernel, out_shape=jax.ShapeDtypeStruct((BR, NW),...]
    all_gather x1 -> x0, waiting for transfers between devices: 69.3 us -> none  [body(): occ_full = lax.all_gather(occ_panel, ('pair', 'orb'), axis=1, tiled=True)]
    psum x1 -> x0, waiting for transfers between devices: 54 us -> none  [body(): occ_half = lax.psum(partial_value.astype(jnp.bfloat16), 'orb')]
    dot_general x3 -> x0, matrix products: 51.2 us -> none  [the longest x1 31.4 us: body(): jnp.einsum('tb,tr,tjrs->jrbs', onehot, row_live, half_terms, precision=la...]
    convert_element_type x1 -> x0, local copies, waits for them, and re-layouts: 6.09 us -> none  [body(): occ_half = lax.psum(partial_value.astype(jnp.bfloat16), 'orb')]
    all_gather x1 -> x0, local copies, waits for them, and re-layouts: 4.28 us -> none  [body(): occ_full = lax.all_gather(occ_panel, ('pair', 'orb'), axis=1, tiled=True)]
    unnamed x5 -> x13, local copies, waits for them, and re-layouts: 4.98 us -> 6.44 us
  transfers between devices with their start and end apart: 3 -> 0, of which waited for: 3 -> 0; matrix products, arithmetic and copies ran while one was open for 1% -> 0% of each run, Pallas kernels for 0% -> 0%
where the time goes in v1:
time: 114 us; the launch traced here: 113 us
  Pallas kernels  107 us (94%)
  local copies, waits for them, and re-layouts  6.44 us (6%)
    pallas_call x1, Pallas kernels, transform(): pl.pallas_call(transform_kernel, out_shape=jax.ShapeDtypeStruct((BR, NW),...  74.8 us
    pallas_call x1, Pallas kernels, gather_panel(): pl.pallas_call(gather_kernel, out_shape=jax.ShapeDtypeStruct((4, 4, 2, 3,...  22.7 us
    pallas_call x1, Pallas kernels, tile_sums(): pl.pallas_call(tiles_kernel, grid_spec=pltpu.PrefetchScalarGridSpec(num_s...  9.55 us
    unnamed x13, local copies, waits for them, and re-layouts  6.44 us

profile of v1, /device:TPU:1, one launch (start us, length us, event | category | flops | bytes accessed | tf_op | source)
XLA Modules:
  0.0 113.5 jit_solution(4026612383681147029)
XLA Ops:
  0.0 0.0 copy-start.1
  0.0 0.7 copy-done.1
  0.7 22.7 %gather_panel.1 = bf16[4,4,2,3,64,128]{5,4,3,2,1,0:T(8,128)(2,1)S(1)} custom-call(bf16[64,96]{1,0:T(8,128)(2,1)S(1)} %copy-done.1), custom_call_target="tpu_custom_call" | custom-call | tf_op jit(solution)/shard_map/gather_panel/pallas_call | solution.py:123
  23.4 0.0 copy-start.2
  23.4 0.6 copy-done.2
  24.1 0.0 copy-start.3
  24.1 0.7 copy-done.3
  24.7 0.0 copy-start.4
  24.7 0.7 copy-done.4
  25.4 0.0 copy-start.5
  25.4 0.7 copy-done.5
  26.0 9.6 %tile_sums.1 = bf16[2560,384]{1,0:T(8,128)(2,1)S(1)} custom-call(s32[12]{0:T(128)S(1)} %copy-done.2, s32[12]{0:T(128)S(1)} %copy-done.3, s32[12]{0:T(128)S(1)} %copy-done.4, s32[12]{0:T(128)S(1)} %copy-done.5, bf16[12,40,128,128]{3,2,1,0:T(8,128)(2,1)} %tile_ref.1, bf16[96,64,128]{2,1,0:T(8,128)(2,1)S(1)} %bitcast.4), custom_call_target="tpu_custom_call" | custom-call | tf_op jit(solution)/shard_map/tile_sums/pallas_call | solution.py:186
  35.6 0.0 copy-start
  35.6 1.3 %copy-done = bf16[2560,384]{1,0:T(8,128)(2,1)} copy-done((bf16[2560,384]{1,0:T(8,128)(2,1)}, bf16[2560,384]{1,0:T(8,128)(2,1)S(1)}, u32[]{:S(2)}) %copy-start) | copy-done | bytes 1966104
  36.9 74.8 %transform.1 = bf16[80,2816]{1,0:T(8,128)(2,1)} custom-call(bf16[16,2,80,384]{3,2,1,0:T(8,128)(2,1)} %bitcast.3, bf16[384,2816]{1,0:T(8,128)(2,1)} %b_ref.1), custom_call_target="tpu_custom_call" | custom-call | tf_op jit(solution)/shard_map/transform/pallas_call | solution.py:467
  111.7 1.8 %copy.9 = bf16[2,40,2816]{2,1,0:T(8,128)(2,1)} copy(bf16[2,40,2816]{2,1,0:T(8,128)(2,1)} %bitcast.5) | data formatting | bytes 901120
Async XLA Ops:
  0.0 0.7 copy-start.1
  23.4 0.7 copy-start.2
  24.1 0.7 copy-start.3
  24.7 0.7 copy-start.4
  25.4 0.7 copy-start.5
  35.6 1.3 %copy-start = (bf16[2560,384]{1,0:T(8,128)(2,1)}, bf16[2560,384]{1,0:T(8,128)(2,1)S(1)}, u32[]{:S(2)}) copy-start(bf16[2560,384]{1,0:T(8,128)(2,1)S(1)} %tile_sums.1) | copy-start | bytes 5898244

commit v2 on v0

v2 whole, which is shorter than its diff:
```python
import jax
import jax.numpy as jnp
from jax import lax
from jax.experimental import pallas as pl
from jax.experimental.pallas import tpu as pltpu
from jax.sharding import PartitionSpec as P

BS = 128
NOCC = 64
ROWS = 40
SLOTS = 12
NBLK = 96
SIG = 3
KW = 384
NW = 2816
HW = NW // 2
CUT = 768
BR = 80
MESH = pl.DeviceIdType.MESH
F32 = jnp.float32
BF16 = jnp.bfloat16

CHUNKS = [
    [(2, 2), (2, 1)],
    [(1, 2), (2, 3)],
    [(3, 2), (2, 0)],
    [(0, 2), (1, 1)],
    [(3, 3), (1, 3)],
    [(3, 1), (1, 0)],
    [(3, 0), (0, 1)],
    [(0, 3), (0, 0)],
]
NC = len(CHUNKS)
AT = {block: (k, i) for k, chunk in enumerate(CHUNKS) for i, block in enumerate(chunk)}


def pair_of(x, y, c):
    return (x * 4 + y) * 2 + c


def push(src, dst, send_sem, recv_sem, pair, z):
    return pltpu.make_async_remote_copy(
        src_ref=src,
        dst_ref=dst,
        send_sem=send_sem,
        recv_sem=recv_sem,
        device_id=(pair, z),
        device_id_type=MESH,
    )


def fused_kernel(
    tiles_hbm, lam_hbm, sig_hbm, rows_hbm, mask_hbm, occ_ref, b_hbm, out_ref,
    tiles, ints, b2, zbuf, gat, lhs, acc, a, zra, zrb, red, a2, cc, r1, r2, r3, r4,
    in_sem, b_sem, gz_s, gz_r, ga_s, ga_r, gc_s, gc_r,
    za_s, za_r, zb_s, zb_r, zc_s, zc_r, zd_s, zd_r,
    r1_s, r1_r, r2_s, r2_r, r3_s, r3_r, r4_s, r4_r,
):
    pair = lax.axis_index("pair")
    z = lax.axis_index("orb")
    x, y, c = pair // 8, (pair // 2) % 4, pair % 2
    other = pair_of(x, y, 1 - c)
    up, down = (z + 1) % 4, (z + 3) % 4
    xs = {1: pair_of((x + 1) % 4, y, c), -1: pair_of((x + 3) % 4, y, c)}
    ys = {1: pair_of(x, (y + 1) % 4, c), -1: pair_of(x, (y + 3) % 4, c)}
    first, second = (xs, ys), (ys, xs)

    own_k = pl.ds(pl.multiple_of(c * KW, BS), KW)
    other_k = pl.ds(pl.multiple_of((1 - c) * KW, BS), KW)
    b_own = pltpu.make_async_copy(b_hbm, b2.at[own_k], b_sem.at[0])
    b_own.start()
    locals_ = []
    for i, ref in enumerate((lam_hbm, sig_hbm, rows_hbm, mask_hbm)):
        locals_.append(pltpu.make_async_copy(ref, ints.at[i], in_sem.at[i]))
    for i in range(4):
        part = pl.ds(3 * i, 3)
        locals_.append(pltpu.make_async_copy(tiles_hbm.at[part], tiles.at[part], in_sem.at[4 + i]))
    for copy in locals_:
        copy.start()

    barrier = pltpu.get_barrier_semaphore()

    def hello(pair_id, z_id):
        pl.semaphore_signal(barrier, inc=1, device_id=(pair_id, z_id), device_id_type=MESH)

    hello(other, z)
    hello(other, up)
    hello(other, down)
    for d in range(1, 4):
        hello(pair_of((x + d) % 4, y, c), z)
        hello(pair_of(x, (y + d) % 4, c), z)
        hello(pair, (z + d) % 4)
    zbuf[z] = jnp.concatenate([occ_ref[...], jnp.zeros((NOCC, 32), BF16)], axis=1)
    lhs[...] = jnp.zeros_like(lhs)
    pl.semaphore_wait(barrier, 12)

    sends = []

    def start(copy):
        copy.start()
        sends.append(copy)
        return copy

    steps = [
        start(push(zbuf.at[z], zbuf.at[z], gz_s.at[d - 1], gz_r.at[d - 1], pair, (z + d) % 4))
        for d in range(1, 4)
    ]
    b_own.wait()
    b_away = start(push(b2.at[own_k], b2.at[own_k], b_sem.at[1], b_sem.at[2], other, z))
    for copy in steps:
        copy.wait_recv()
    whole = jnp.concatenate([zbuf[i][:, :96] for i in range(4)], axis=1)
    for k in range(3):
        gat[x, y, c, k] = whole[:, k * BS : (k + 1) * BS]
    lo, hi = pl.ds(0, 32), pl.ds(32, 32)
    first_a, first_b = [], []
    for d in range(1, 4):
        view = gat.at[x, y, c, :, lo]
        first_a.append(
            start(push(view, view, ga_s.at[0, d - 1], ga_r.at[0, d - 1], pair_of((x + d) % 4, y, c), z))
        )
        view = gat.at[x, y, c, :, hi]
        first_b.append(
            start(push(view, view, ga_s.at[1, d - 1], ga_r.at[1, d - 1], pair_of(x, (y + d) % 4, c), z))
        )
    for copy in first_a:
        copy.wait_recv()
    second_a, second_b, across = [], [], []
    row = gat.at[:, y, c, :, lo]
    for d in range(1, 4):
        second_a.append(
            start(push(row, row, ga_s.at[2, d - 1], ga_r.at[2, d - 1], pair_of(x, (y + d) % 4, c), z))
        )
    across.append(start(push(row, row, gc_s.at[0, 0], gc_r.at[0, 0], other, z)))
    for copy in first_b:
        copy.wait_recv()
    col = gat.at[x, :, c, :, hi]
    for d in range(1, 4):
        second_b.append(
            start(push(col, col, ga_s.at[3, d - 1], ga_r.at[3, d - 1], pair_of((x + d) % 4, y, c), z))
        )
    across.append(start(push(col, col, gc_s.at[1, 0], gc_r.at[1, 0], other, z)))
    for d in range(1, 4):
        second_a[d - 1].wait_recv()
        row = gat.at[:, (y - d + 4) % 4, c, :, lo]
        across.append(start(push(row, row, gc_s.at[0, d], gc_r.at[0, d], other, z)))
        second_b[d - 1].wait_recv()
        col = gat.at[(x - d + 4) % 4, :, c, :, hi]
        across.append(start(push(col, col, gc_s.at[1, d], gc_r.at[1, d], other, z)))
    for copy in across:
        copy.wait_recv()
    for copy in locals_:
        copy.wait()

    for t in range(SLOTS):
        lam = ints[0, t]
        picked = gat[lam // 24, (lam // 6) % 4, (lam // 3) % 2, lam % 3]
        for s in range(SIG):
            keep = jnp.logical_and(ints[1, t] == s, ints[3, t] > 0)
            lhs[s * NOCC : (s + 1) * NOCC, t * BS : (t + 1) * BS] = jnp.where(
                keep, picked, jnp.zeros_like(picked)
            )

    @pl.loop(0, ROWS // 2, unroll=4)
    def _(q):
        parts = []
        for t in range(SLOTS):
            both = []
            for i in range(2):
                tile = tiles[t, 2 * q + i]
                both.append(jnp.where(2 * q + i < ints[2, t], tile, jnp.zeros_like(tile)))
            parts.append(jnp.concatenate(both, axis=1))
        got = jnp.dot(lhs[...], jnp.concatenate(parts, axis=0), preferred_element_type=F32)
        for i in range(2):
            for s in range(SIG):
                acc[s, pl.ds(2 * q + i, NOCC, stride=ROWS), :] = got[
                    s * NOCC : (s + 1) * NOCC, i * BS : (i + 1) * BS
                ]

    def z_load(k):
        for i, (dx, dy) in enumerate(CHUNKS[k]):
            for core in range(2):
                at = pl.multiple_of(pair_of((x + dx) % 4, (y + dy) % 4, core) * BR, 16)
                for s in range(SIG):
                    a[k, 2 * i + core, :, s * BS : (s + 1) * BS] = acc[s, pl.ds(at, BR), :].astype(BF16)

    def cut(k, d):
        return (0, 48 - 16 * (k % 2)) if d == 1 else (48 - 16 * (k % 2), BR)

    def far_copy(k, d):
        lo, hi = cut(k, d)
        i = 0 if d == 1 else 1
        span = pl.ds(lo, hi - lo)
        return push(
            a.at[k, (z + 2) % 4, span], zra.at[k, span], za_s.at[k, i], za_r.at[k, i], pair, (z + d) % 4
        )

    def near_copy(k, d):
        i = 0 if d == 1 else 1
        return push(a.at[k, (z + d) % 4], zrb.at[k, i], zb_s.at[k, i], zb_r.at[k, i], pair, (z + d) % 4)

    def z_far(k):
        z_load(k)
        for d in (1, -1):
            start(far_copy(k, d))

    def z_near(k):
        for d in (1, -1):
            far_copy(k, d).wait_recv()
            unit = (z + d) % 4
            for r in range(*cut(k, d), 16):
                a[k, unit, r : r + 16] = (
                    a[k, unit, r : r + 16].astype(F32) + zra[k, r : r + 16].astype(F32)
                ).astype(BF16)
            start(near_copy(k, d))

    mine = z % 2 == c

    def out_copy(k, i):
        target, zt = ((other, z), (jnp.where(mine, pair, other), up), (jnp.where(mine, pair, other), down))[i]
        return push(red.at[k], a2.at[k, c, z // 2], zc_s.at[k, i], zc_r.at[k, c, i], target, zt)

    def z_sum(k):
        for d in (1, -1):
            near_copy(k, d).wait_recv()
        for r in range(0, BR, 16):
            red[k, r : r + 16] = (
                a[k, z, r : r + 16].astype(F32)
                + zrb[k, 0, r : r + 16].astype(F32)
                + zrb[k, 1, r : r + 16].astype(F32)
            ).astype(BF16)
        start(out_copy(k, 1))
        start(out_copy(k, 2))

        @pl.when(mine)
        def _():
            a2[k, c, z // 2] = red[k]

        @pl.when(jnp.logical_not(mine))
        def _():
            out_copy(k, 0).start()

    def landed(k, core, zf, i):
        view = a2.at[k, core, zf // 2]
        return push(view, view, zc_s.at[k, i], zc_r.at[k, core, i], other, z)

    def on_copy(k, core):
        zf, zt = (down, up) if core == 0 else (up, down)
        view = a2.at[k, core, zf // 2]
        return push(view, view, zd_s.at[k, core], zd_r.at[k, core], pair, zt)

    def z_on(k):
        @pl.when(jnp.logical_not(mine))
        def _():
            for core, zf, i in ((0, down, 1), (1, up, 2)):
                landed(k, core, zf, i).wait_recv()
                on_copy(k, core).start()

    def z_end(k):
        @pl.when(mine)
        def _():
            landed(k, 1 - c, z, 0).wait_recv()
            for core in range(2):
                view = a2.at[k, core, ((z + 2) % 4) // 2]
                push(view, view, zd_s.at[k, core], zd_r.at[k, core], other, z).wait_recv()

        @pl.when(jnp.logical_not(mine))
        def _():
            landed(k, 1, down, 1).wait_recv()
            landed(k, 0, up, 2).wait_recv()

    def multiply(k):
        left = jnp.concatenate([a2[k, i].reshape(2 * BR, KW) for i in range(2)], axis=1)
        for h in range(2):
            for at in range(0, HW, 512):
                width = min(512, HW - at)
                got = jnp.dot(
                    left, b2[:, h * HW + at : h * HW + at + width], preferred_element_type=F32
                )
                cc[k, h, :, :, at : at + width] = got.astype(BF16).reshape(2, BR, width)

    def held(h, f, s):
        k, i = AT[(f, s) if h == 0 else (s, f)]
        return cc.at[k, h, i]

    def add(into, terms, lo=0, hi=HW, out=None):
        for r in range(0, BR, 16):
            total = into[r : r + 16, lo:hi].astype(F32)
            for term in terms:
                total = total + term[r : r + 16, lo:hi].astype(F32)
            if out is None:
                into[r : r + 16, lo:hi] = total.astype(BF16)
            else:
                out_ref[r : r + 16, out : out + hi - lo] = total.astype(BF16)

    def columns(d):
        return pl.ds(0, CUT) if d == 1 else pl.ds(CUT, HW - CUT)

    def far(src, dst, send_sem, recv_sem, to):
        for i, d in enumerate((1, -1)):
            start(push(src.at[:, columns(d)], dst.at[:, columns(d)], send_sem.at[i], recv_sem.at[i], to[d], z))

    def near(block, d, far_dst, far_s, far_r, dst, send_sem, recv_sem, to):
        i = 0 if d == 1 else 1
        view = far_dst.at[:, columns(d)]
        push(view, view, far_s.at[i], far_r.at[i], to[d], z).wait_recv()
        add(block, [far_dst], 0 if d == 1 else CUT, CUT if d == 1 else HW)
        start(push(block, dst.at[i], send_sem.at[i], recv_sem.at[i], to[d], z))

    def arrived(dst, send_sem, recv_sem):
        for i in range(2):
            push(dst.at[i], dst.at[i], send_sem.at[i], recv_sem.at[i], other, z).wait_recv()

    def far1(h, s):
        far(held(h, 2, s), r1.at[h, s], r1_s.at[h, s], r1_r.at[h, s], first[h])

    def near1(h, s, d):
        near(
            held(h, d % 4, s), d, r1.at[h, s], r1_s.at[h, s], r1_r.at[h, s],
            r2.at[h, s], r2_s.at[h, s], r2_r.at[h, s], first[h],
        )

    def home1(h, s):
        arrived(r2.at[h, s], r2_s.at[h, s], r2_r.at[h, s])
        add(held(h, 0, s), [r2.at[h, s, 0], r2.at[h, s, 1]])

    def far2(h):
        far(held(h, 0, 2), r3.at[h], r3_s.at[h], r3_r.at[h], second[h])

    def near2(h, d):
        near(
            held(h, 0, d % 4), d, r3.at[h], r3_s.at[h], r3_r.at[h], r4.at[h], r4_s.at[h], r4_r.at[h], second[h]
        )

    def final(h):
        arrived(r4.at[h], r4_s.at[h], r4_r.at[h])
        add(held(h, 0, 0), [r4.at[h, 0], r4.at[h, 1]], out=h * HW)

    def pair_steps(k):
        if k == 0:
            far1(0, 2)
            far1(1, 2)
            far1(0, 1)
        if k == 1:
            far1(0, 3)
            far1(1, 1)
            near1(1, 2, 1)
            near1(0, 2, 1)
            near1(1, 2, -1)
        if k == 2:
            far1(0, 0)
            far1(1, 3)
            near1(0, 2, -1)
        if k == 3:
            far1(1, 0)
            near1(0, 1, 1)
            near1(1, 1, 1)
            home1(1, 2)
            far2(1)
        if k == 4:
            near1(0, 3, -1)
            near1(1, 3, -1)
            near1(0, 3, 1)
            near1(1, 1, -1)
            home1(0, 2)
            far2(0)
        if k == 5:
            near1(0, 1, -1)
            near1(1, 3, 1)
            near1(0, 0, 1)
        if k == 6:
            near1(0, 0, -1)
            near1(1, 0, 1)
            home1(1, 1)
            near2(1, 1)
        if k == 7:
            near1(1, 0, -1)
            home1(0, 1)
            near2(0, 1)
            home1(1, 3)
            near2(1, -1)
            home1(0, 3)
            near2(0, -1)
            home1(0, 0)
            home1(1, 0)
            final(1)
            final(0)

    z_far(0)
    for t in range(NC + 3):
        if t + 1 < NC:
            z_far(t + 1)
        if t < NC:
            z_near(t)
        if 0 <= t - 1 < NC:
            z_sum(t - 1)
        if 0 <= t - 2 < NC:
            z_on(t - 2)
        if t == 2:
            push(b2.at[other_k], b2.at[other_k], b_sem.at[1], b_sem.at[2], other, z).wait_recv()
        if t >= 3:
            z_end(t - 3)
            multiply(t - 3)
            pair_steps(t - 3)

    for copy in sends:
        copy.wait_send()
    for k in range(NC):

        @pl.when(jnp.logical_not(mine))
        def _():
            out_copy(k, 0).wait_send()
            for core in range(2):
                on_copy(k, core).wait_send()


def fused(tiles, lam, sig, rows, mask, occ, b):
    sem = pltpu.SemaphoreType.DMA

    def vm(*shape):
        return pltpu.VMEM(shape, BF16)

    def twice(*shapes):
        return [sem(shape) for shape in shapes for _ in range(2)]

    hbm = pl.BlockSpec(memory_space=pl.ANY)
    vmem = pl.BlockSpec(memory_space=pltpu.VMEM)
    return pl.pallas_call(
        fused_kernel,
        out_shape=jax.ShapeDtypeStruct((BR, NW), BF16),
        in_specs=[hbm, hbm, hbm, hbm, hbm, vmem, hbm],
        out_specs=vmem,
        scratch_shapes=[
            vm(SLOTS, ROWS, BS, BS),
            pltpu.SMEM((4, SLOTS), jnp.int32),
            vm(2 * KW, NW),
            vm(4, NOCC, BS),
            vm(4, 4, 2, 3, NOCC, BS),
            vm(SIG * NOCC, SLOTS * BS),
            pltpu.VMEM((SIG, NOCC * ROWS, BS), F32),
            vm(NC, 4, BR, KW),
            vm(NC, BR, KW),
            vm(NC, 2, BR, KW),
            vm(NC, BR, KW),
            vm(NC, 2, 2, BR, KW),
            vm(NC, 2, 2, BR, HW),
            vm(2, 4, BR, HW),
            vm(2, 4, 2, BR, HW),
            vm(2, BR, HW),
            vm(2, 2, BR, HW),
            sem((8,)),
            sem((3,)),
            *twice((3,), (4, 3), (2, 4)),
            *twice((NC, 2), (NC, 2)),
            sem((NC, 3)),
            sem((NC, 2, 3)),
            *twice((NC, 2), (2, 4, 2), (2, 4, 2), (2, 2), (2, 2)),
        ],
        compiler_params=pltpu.CompilerParams(
            collective_id=0, has_side_effects=True, vmem_limit_bytes=60 * 2**20
        ),
        name="fused",
    )(tiles, lam, sig, rows, mask, occ, b)


def body(integral_tiles, tile_lam, tile_sig, tile_rows, screen_mask, occ_panel, virt_panel):
    out = fused(
        integral_tiles, tile_lam, tile_sig, tile_rows, screen_mask, occ_panel, virt_panel
    )
    return out.reshape(2, ROWS, NW)


def solution(mesh):
    return jax.shard_map(
        body,
        mesh=mesh,
        in_specs=(
            P(("pair", "orb"), None, None, None),
            P(("pair", "orb")),
            P(("pair", "orb")),
            P(("pair", "orb")),
            P(("pair", "orb")),
            P(None, ("pair", "orb")),
            P("pair", "orb"),
        ),
        out_specs=P("pair", None, "orb"),
        check_vma=False,
    )
```

time: 320 us -> 88.2 us (0.28)
  waiting for transfers between devices: 232 us -> 0 us
  Pallas kernels: 0 us -> 85.9 us
  matrix products: 51.2 us -> 0 us
  local copies, waits for them, and re-layouts: 20.4 us -> 1.81 us
  between operations: 13.1 us -> 0.01 us
    reduce_scatter x1 -> x0, waiting for transfers between devices: 108 us -> none  [body(): lax.psum_scatter(product.reshape(lax.axis_size('pair') * owned_rows, row_...]
    pallas_call x0 -> x1, Pallas kernels: none -> 85.9 us  [fused(): pl.pallas_call(fused_kernel, out_shape=jax.ShapeDtypeStruct((BR, NW), BF1...]
    all_gather x1 -> x0, waiting for transfers between devices: 69.3 us -> none  [body(): occ_full = lax.all_gather(occ_panel, ('pair', 'orb'), axis=1, tiled=True)]
    psum x1 -> x0, waiting for transfers between devices: 54 us -> none  [body(): occ_half = lax.psum(partial_value.astype(jnp.bfloat16), 'orb')]
    dot_general x3 -> x0, matrix products: 51.2 us -> none  [the longest x1 31.4 us: body(): jnp.einsum('tb,tr,tjrs->jrbs', onehot, row_live, half_terms, precision=la...]
    convert_element_type x1 -> x0, local copies, waits for them, and re-layouts: 6.09 us -> none  [body(): occ_half = lax.psum(partial_value.astype(jnp.bfloat16), 'orb')]
    all_gather x1 -> x0, local copies, waits for them, and re-layouts: 4.28 us -> none  [body(): occ_full = lax.all_gather(occ_panel, ('pair', 'orb'), axis=1, tiled=True)]
  transfers between devices with their start and end apart: 3 -> 0, of which waited for: 3 -> 0; matrix products, arithmetic and copies ran while one was open for 1% -> 0% of each run, Pallas kernels for 0% -> 0%
where the time goes in v2:
time: 88.2 us; the launch traced here: 87.7 us
  Pallas kernels  85.9 us (97%)
  local copies, waits for them, and re-layouts  1.81 us (2%)
    pallas_call x1, Pallas kernels, fused(): pl.pallas_call(fused_kernel, out_shape=jax.ShapeDtypeStruct((BR, NW), BF1...  85.9 us
    unnamed x1, local copies, waits for them, and re-layouts  1.81 us

profile of v2, /device:TPU:1, one launch (start us, length us, event | category | flops | bytes accessed | tf_op | source)
XLA Modules:
  0.0 87.7 jit_solution(3156590930696659684)
XLA Ops:
  0.0 85.9 %fused.1 = bf16[80,2816]{1,0:T(8,128)(2,1)} custom-call(bf16[12,40,128,128]{3,2,1,0:T(8,128)(2,1)} %tiles_hbm.1, s32[12]{0:T(128)} %lam_hbm.1, s32[12]{0:T(128)} %sig_hbm.1, s32[12]{0:T(128)} %rows_hbm.1, s32[12]{0:T(128)} %mask_hbm.1, bf16[64,96]{1,0:T(8,128)(2,1)} %occ_ref.1, bf16[384,2816]{1,0:T(8,128)(2,1)} %b_hbm.1), custom_call_target="tpu_custom_call" | custom-call | tf_op jit(solution)/shard_map/fused/pallas_call | solution.py:428
  85.9 1.8 %copy.9 = bf16[2,40,2816]{2,1,0:T(8,128)(2,1)} copy(bf16[2,40,2816]{2,1,0:T(8,128)(2,1)} %bitcast.1) | data formatting | bytes 901120

commit v3 on v2

v3 whole, which is shorter than its diff:
```python
import jax
import jax.numpy as jnp
from jax import lax
from jax.experimental import pallas as pl
from jax.experimental.pallas import tpu as pltpu
from jax.sharding import PartitionSpec as P

BS = 128
NOCC = 64
ROWS = 40
SLOTS = 12
NBLK = 96
SIG = 3
KW = 384
NW = 2816
HW = NW // 2
CUT = 768
BR = 80
MESH = pl.DeviceIdType.MESH
F32 = jnp.float32
BF16 = jnp.bfloat16

CHUNKS = [
    [[((2, 1), 0, BR)], [((1, 2), 0, BR)]],
    [[((2, 3), 0, BR)], [((3, 2), 0, BR)]],
    [[((1, 1), 0, 48), ((3, 3), 0, 32)], [((2, 2), 0, BR)]],
    [[((1, 3), 0, BR)], [((3, 1), 0, BR)]],
    [[((0, 3), 0, 32), ((3, 0), 0, 48)], [((2, 0), 0, BR)]],
    [[((1, 1), 48, BR), ((3, 3), 32, BR)], [((0, 2), 0, BR)]],
    [[((0, 1), 0, BR)], [((1, 0), 0, BR)]],
    [[((0, 3), 32, BR), ((3, 0), 48, BR)], [((0, 0), 0, BR)]],
]
NC = len(CHUNKS)
DIRECT = 3

ORDER = [
    ("zf", 0), ("zf", 1), ("zf", 2), ("zs", 0), ("zf", 3), ("zs", 1), ("zf", 4), ("zs", 2), ("zf", 5), ("mm", 0),
    ("f1", 0, 1), ("f1", 1, 1), ("zn", 3), ("mm", 1), ("f1", 0, 3), ("f1", 1, 3), ("zn", 4), ("mm", 2),
    ("f1", 0, 2), ("f1", 1, 2), ("zn", 5), ("n1", 0, 1, 1, 0), ("n1", 1, 1, 1, 0), ("zs", 3), ("n1", 0, 3, -1, 0),
    ("n1", 1, 3, -1, 0), ("zs", 4), ("zs", 5), ("n1", 0, 2, -1, 0), ("n1", 1, 2, -1, 0), ("n1", 0, 2, 1, 0),
    ("n1", 1, 2, 1, 0), ("zo", 3), ("zf", 6), ("zo", 4), ("zf", 7), ("zo", 5), ("mm", 3), ("zn", 6),
    ("n1", 0, 1, -1, 0), ("n1", 0, 3, 1, 0), ("n1", 1, 1, -1, 0), ("zn", 7), ("n1", 1, 3, 1, 0), ("mm", 4),
    ("f1", 0, 0), ("mm", 5), ("f1", 1, 0), ("zs", 6), ("n1", 0, 1, 1, 1), ("n1", 0, 3, -1, 1), ("n1", 1, 1, 1, 1),
    ("zs", 7), ("n1", 1, 3, -1, 1), ("h1", 0, 2, 0), ("f2", 0), ("h1", 1, 2, 0), ("f2", 1), ("zo", 6), ("zo", 7),
    ("n1", 0, 0, -1, 0), ("n1", 1, 0, -1, 0), ("mm", 6), ("n1", 0, 0, 1, 0), ("n1", 1, 0, 1, 0), ("mm", 7),
    ("n1", 0, 0, -1, 1), ("n1", 1, 0, -1, 1), ("h1", 0, 1, 0), ("h1", 0, 3, 0), ("h1", 0, 3, 1), ("h1", 1, 1, 0),
    ("h1", 1, 3, 0), ("h1", 1, 3, 1), ("n2", 1, -1, 0), ("n2", 1, -1, 1), ("n2", 0, -1, 0), ("n2", 0, -1, 1),
    ("n2", 1, 1, 0), ("n2", 0, 1, 0), ("h1", 0, 0, 0), ("h1", 1, 0, 0), ("fi", 1), ("fi", 0),
]


def pieces():
    found = {}
    for k, chunk in enumerate(CHUNKS):
        for i, parts in enumerate(chunk):
            at = 0
            for block, lo, hi in parts:
                found.setdefault(block, []).append((k, i, at, lo, hi))
                at += hi - lo
    return found


PIECES = pieces()


def pair_of(x, y, c):
    return (x * 4 + y) * 2 + c


def push(src, dst, send_sem, recv_sem, pair, z):
    return pltpu.make_async_remote_copy(
        src_ref=src,
        dst_ref=dst,
        send_sem=send_sem,
        recv_sem=recv_sem,
        device_id=(pair, z),
        device_id_type=MESH,
    )


def fused_kernel(
    tiles_hbm, lam_hbm, sig_hbm, rows_hbm, mask_hbm, occ_hbm, b_hbm, out_ref,
    tiles, ints, b2, panel, zbuf, gat, lhs, acc, a, zra, zrb, zdx, red, a2, cc, r1, r2, r3, r4,
    in_sem, b_sem, gz_s, gz_r, ga_s, ga_r, gs_s, gs_r, gc_s, gc_r,
    za_s, za_r, zb_s, zb_r, ze_s, ze_r, zc_s, zc_r, zd_s, zd_r,
    r1_s, r1_r, r2_s, r2_r, r3_s, r3_r, r4_s, r4_r,
):
    pair = lax.axis_index("pair")
    z = lax.axis_index("orb")
    x, y, c = pair // 8, (pair // 2) % 4, pair % 2
    other = pair_of(x, y, 1 - c)
    up, down = (z + 1) % 4, (z + 3) % 4
    xs = {1: pair_of((x + 1) % 4, y, c), -1: pair_of((x + 3) % 4, y, c)}
    ys = {1: pair_of(x, (y + 1) % 4, c), -1: pair_of(x, (y + 3) % 4, c)}
    axes1, axes2 = (xs, ys), (ys, xs)

    own_k = pl.ds(pl.multiple_of(c * KW, BS), KW)
    other_k = pl.ds(pl.multiple_of((1 - c) * KW, BS), KW)
    occ_own = pltpu.make_async_copy(occ_hbm, panel, b_sem.at[3])
    occ_own.start()
    b_own = pltpu.make_async_copy(b_hbm, b2.at[own_k], b_sem.at[0])
    locals_ = []
    for i, ref in enumerate((lam_hbm, sig_hbm, rows_hbm, mask_hbm)):
        locals_.append(pltpu.make_async_copy(ref, ints.at[i], in_sem.at[i]))
    for i in range(4):
        part = pl.ds(3 * i, 3)
        locals_.append(pltpu.make_async_copy(tiles_hbm.at[part], tiles.at[part], in_sem.at[4 + i]))
    for copy in locals_:
        copy.start()
    b_own.start()

    barrier = pltpu.get_barrier_semaphore()

    def hello(pair_id, z_id):
        pl.semaphore_signal(barrier, inc=1, device_id=(pair_id, z_id), device_id_type=MESH)

    hello(other, z)
    hello(other, up)
    hello(other, down)
    for d in range(1, 4):
        hello(pair_of((x + d) % 4, y, c), z)
        hello(pair_of(x, (y + d) % 4, c), z)
        hello(pair, (z + d) % 4)
    occ_own.wait()
    zbuf[z] = jnp.concatenate([panel[...], jnp.zeros((NOCC, 32), BF16)], axis=1)
    pl.semaphore_wait(barrier, 12)

    sends = []

    def start(copy):
        copy.start()
        sends.append(copy)
        return copy

    steps = [
        start(push(zbuf.at[z], zbuf.at[z], gz_s.at[d - 1], gz_r.at[d - 1], pair, (z + d) % 4))
        for d in range(1, 4)
    ]
    for copy in steps:
        copy.wait_recv()
    whole = jnp.concatenate([zbuf[i][:, :96] for i in range(4)], axis=1)
    for k in range(3):
        gat[x, y, c, k] = whole[:, k * BS : (k + 1) * BS]
    spans = (pl.ds(0, 32), pl.ds(32, 32))

    def block(half, f, s):
        bx, by = ((x - f + 4) % 4, (y - s + 4) % 4) if half == 0 else ((x - s + 4) % 4, (y - f + 4) % 4)
        return gat.at[bx, by, c, :, spans[half]]

    def along(axis, d):
        return pair_of((x + d) % 4, y, c) if axis == 0 else pair_of(x, (y + d) % 4, c)

    def second(half, f):
        view = block(half, f, 0)
        for d in range(1, 4):
            start(push(view, view, gs_s.at[half, f, d - 1], gs_r.at[half, f, d - 1], along(1 - half, d), z))
        start(push(view, view, gc_s.at[half, f, 0], gc_r.at[half, f, 0], other, z))

    for d in (1, 3, 2):
        for half in range(2):
            view = block(half, 0, 0)
            start(push(view, view, ga_s.at[half, d - 1], ga_r.at[half, d - 1], along(half, d), z))
    for half in range(2):
        second(half, 0)
    for f in (1, 3, 2):
        for half in range(2):
            view = block(half, f, 0)
            push(view, view, ga_s.at[half, f - 1], ga_r.at[half, f - 1], other, z).wait_recv()
            second(half, f)
    for f in (0, 1, 3, 2):
        for d in (1, 3, 2):
            for half in range(2):
                view = block(half, f, d)
                push(view, view, gs_s.at[half, f, d - 1], gs_r.at[half, f, d - 1], other, z).wait_recv()
                start(push(view, view, gc_s.at[half, f, d], gc_r.at[half, f, d], other, z))
    for half in range(2):
        for f in range(4):
            for d in range(4):
                bx, by = ((x - f + 4) % 4, (y - d + 4) % 4) if half == 0 else ((x - d + 4) % 4, (y - f + 4) % 4)
                view = gat.at[bx, by, 1 - c, :, spans[half]]
                push(view, view, gc_s.at[half, f, d], gc_r.at[half, f, d], other, z).wait_recv()
    for copy in locals_:
        copy.wait()
    b_own.wait()
    start(push(b2.at[own_k], b2.at[own_k], b_sem.at[1], b_sem.at[2], other, z))

    for t in range(SLOTS):
        lam = ints[0, t]
        picked = gat[lam // 24, (lam // 6) % 4, (lam // 3) % 2, lam % 3]
        for s in range(SIG):
            keep = jnp.logical_and(ints[1, t] == s, ints[3, t] > 0)
            lhs[s * NOCC : (s + 1) * NOCC, t * BS : (t + 1) * BS] = jnp.where(
                keep, picked, jnp.zeros_like(picked)
            )

    @pl.loop(0, ROWS // 2, unroll=4)
    def _(q):
        parts = []
        for t in range(SLOTS):
            both = []
            for i in range(2):
                tile = tiles[t, 2 * q + i]
                both.append(jnp.where(2 * q + i < ints[2, t], tile, jnp.zeros_like(tile)))
            parts.append(jnp.concatenate(both, axis=1))
        got = jnp.dot(lhs[...], jnp.concatenate(parts, axis=0), preferred_element_type=F32)
        for i in range(2):
            for s in range(SIG):
                acc[s, pl.ds(2 * q + i, NOCC, stride=ROWS), :] = got[
                    s * NOCC : (s + 1) * NOCC, i * BS : (i + 1) * BS
                ]

    def z_load(k):
        for i in range(2):
            to = 0
            for (dx, dy), lo, hi in CHUNKS[k][i]:
                for core in range(2):
                    at = pl.multiple_of(pair_of((x + dx) % 4, (y + dy) % 4, core) * BR + lo, 16)
                    for s in range(SIG):
                        a[k, 2 * i + core, to : to + hi - lo, s * BS : (s + 1) * BS] = acc[
                            s, pl.ds(at, hi - lo), :
                        ].astype(BF16)
                to += hi - lo

    def cut(k, d):
        return (0, 48 - 16 * (k % 2)) if d == 1 else (48 - 16 * (k % 2), BR)

    def far_copy(k, d):
        lo, hi = cut(k, d)
        i = 0 if d == 1 else 1
        span = pl.ds(lo, hi - lo)
        return push(
            a.at[k, (z + 2) % 4, span], zra.at[k, span], za_s.at[k, i], za_r.at[k, i], pair, (z + d) % 4
        )

    def near_copy(k, d):
        i = 0 if d == 1 else 1
        return push(a.at[k, (z + d) % 4], zrb.at[k, i], zb_s.at[k, i], zb_r.at[k, i], pair, (z + d) % 4)

    def direct_copy(k, d):
        return push(
            a.at[k, (z + d) % 4], zdx.at[k, d - 1], ze_s.at[k, d - 1], ze_r.at[k, d - 1], pair, (z + d) % 4
        )

    def z_far(k):
        z_load(k)
        if k < DIRECT:
            for d in (1, 3, 2):
                start(direct_copy(k, d))
            return
        for d in (1, -1):
            start(far_copy(k, d))

    def z_near(k):
        if k < DIRECT:
            return
        for d in (1, -1):
            far_copy(k, d).wait_recv()
            unit = (z + d) % 4
            for r in range(*cut(k, d), 16):
                a[k, unit, r : r + 16] = (
                    a[k, unit, r : r + 16].astype(F32) + zra[k, r : r + 16].astype(F32)
                ).astype(BF16)
            start(near_copy(k, d))

    mine = z % 2 == c

    def out_copy(k, i):
        target, zt = (other, z) if i == 0 else (jnp.where(mine, pair, other), (z + (0, 1, 3, 2)[i]) % 4)
        return push(red.at[k], a2.at[k, c, z // 2], zc_s.at[k, i], zc_r.at[k, c, i], target, zt)

    def z_sum(k):
        if k < DIRECT:
            terms = [zdx.at[k, i] for i in range(3)]
            for d in (1, 3, 2):
                direct_copy(k, d).wait_recv()
        else:
            terms = [zrb.at[k, i] for i in range(2)]
            for d in (1, -1):
                near_copy(k, d).wait_recv()
        for r in range(0, BR, 16):
            total = a[k, z, r : r + 16].astype(F32)
            for term in terms:
                total = total + term[r : r + 16].astype(F32)
            red[k, r : r + 16] = total.astype(BF16)
        start(out_copy(k, 1))
        start(out_copy(k, 2))
        if k < DIRECT:
            start(out_copy(k, 3))

        @pl.when(mine)
        def _():
            a2[k, c, z // 2] = red[k]

        @pl.when(jnp.logical_not(mine))
        def _():
            out_copy(k, 0).start()

    def landed(k, core, zf, i):
        view = a2.at[k, core, zf // 2]
        return push(view, view, zc_s.at[k, i], zc_r.at[k, core, i], other, z)

    def on_copy(k, core):
        zf, zt = (down, up) if core == 0 else (up, down)
        view = a2.at[k, core, zf // 2]
        return push(view, view, zd_s.at[k, core], zd_r.at[k, core], pair, zt)

    def z_on(k):
        if k < DIRECT:
            return

        @pl.when(jnp.logical_not(mine))
        def _():
            for core, zf, i in ((0, down, 1), (1, up, 2)):
                landed(k, core, zf, i).wait_recv()
                on_copy(k, core).start()

    def z_end(k):
        @pl.when(mine)
        def _():
            landed(k, 1 - c, z, 0).wait_recv()
            for core in range(2):
                if k < DIRECT:
                    landed(k, core, (z + 2) % 4, 3).wait_recv()
                else:
                    view = a2.at[k, core, ((z + 2) % 4) // 2]
                    push(view, view, zd_s.at[k, core], zd_r.at[k, core], other, z).wait_recv()

        @pl.when(jnp.logical_not(mine))
        def _():
            landed(k, 1, down, 1).wait_recv()
            landed(k, 0, up, 2).wait_recv()
            if k < DIRECT:
                landed(k, 0, down, 1).wait_recv()
                landed(k, 1, up, 2).wait_recv()

    def multiply(k):
        left = jnp.concatenate([a2[k, i].reshape(2 * BR, KW) for i in range(2)], axis=1)
        for h in range(2):
            for at in range(0, HW, 512):
                width = min(512, HW - at)
                got = jnp.dot(
                    left, b2[:, h * HW + at : h * HW + at + width], preferred_element_type=F32
                )
                cc[k, h, :, :, at : at + width] = got.astype(BF16).reshape(2, BR, width)

    def held(h, f, s, p=0):
        k, i, at, lo, hi = PIECES[(f, s) if h == 0 else (s, f)][p]
        return cc.at[k, h, i, pl.ds(at, hi - lo)], lo, hi

    def add(into, terms, lo=0, hi=HW, out=None):
        for r in range(0, into.shape[0], 16):
            total = into[r : r + 16, lo:hi].astype(F32)
            for term in terms:
                total = total + term[r : r + 16, lo:hi].astype(F32)
            if out is None:
                into[r : r + 16, lo:hi] = total.astype(BF16)
            else:
                out_ref[r : r + 16, out : out + hi - lo] = total.astype(BF16)

    def columns(d):
        return pl.ds(0, CUT) if d == 1 else pl.ds(CUT, HW - CUT)

    def far(src, dst, send_sem, recv_sem, to):
        for i, d in enumerate((1, -1)):
            start(push(src.at[:, columns(d)], dst.at[:, columns(d)], send_sem.at[i], recv_sem.at[i], to[d], z))

    def near(block, p, d, far_dst, far_s, far_r, dst, send_sem, recv_sem, to):
        i = 0 if d == 1 else 1
        ref, lo, hi = block
        if p == 0:
            view = far_dst.at[:, columns(d)]
            push(view, view, far_s.at[i], far_r.at[i], to[d], z).wait_recv()
        span = pl.ds(lo, hi - lo)
        add(ref, [far_dst.at[span]], 0 if d == 1 else CUT, CUT if d == 1 else HW)
        start(push(ref, dst.at[i, span], send_sem.at[i, p], recv_sem.at[i, p], to[d], z))

    def arrived(dst, send_sem, recv_sem, blocks):
        for i in range(2):
            for p, (_, _, _, lo, hi) in enumerate(PIECES[blocks[i]]):
                view = dst.at[i, pl.ds(lo, hi - lo)]
                push(view, view, send_sem.at[i, p], recv_sem.at[i, p], other, z).wait_recv()

    def named(h, f, s):
        return (f, s) if h == 0 else (s, f)

    def far1(h, s):
        far(held(h, 2, s)[0], r1.at[h, s], r1_s.at[h, s], r1_r.at[h, s], axes1[h])

    def near1(h, s, d, p=0):
        near(
            held(h, d % 4, s, p), p, d, r1.at[h, s], r1_s.at[h, s], r1_r.at[h, s],
            r2.at[h, s], r2_s.at[h, s], r2_r.at[h, s], axes1[h],
        )

    def home1(h, s, p=0):
        if p == 0:
            arrived(r2.at[h, s], r2_s.at[h, s], r2_r.at[h, s], [named(h, 1, s), named(h, 3, s)])
        ref, lo, hi = held(h, 0, s, p)
        add(ref, [r2.at[h, s, i, pl.ds(lo, hi - lo)] for i in range(2)])

    def far2(h):
        far(held(h, 0, 2)[0], r3.at[h], r3_s.at[h], r3_r.at[h], axes2[h])

    def near2(h, d, p=0):
        near(
            held(h, 0, d % 4, p), p, d, r3.at[h], r3_s.at[h], r3_r.at[h],
            r4.at[h], r4_s.at[h], r4_r.at[h], axes2[h],
        )

    def final(h):
        arrived(r4.at[h], r4_s.at[h], r4_r.at[h], [named(h, 0, 1), named(h, 0, 3)])
        add(held(h, 0, 0)[0], [r4.at[h, 0], r4.at[h, 1]], out=h * HW)

    def b_wait():
        push(b2.at[other_k], b2.at[other_k], b_sem.at[1], b_sem.at[2], other, z).wait_recv()

    def first_multiply(k):
        if k == 0:
            b_wait()
        z_end(k)
        multiply(k)

    steps = {
        "zf": z_far, "zn": z_near, "zs": z_sum, "zo": z_on, "mm": first_multiply,
        "f1": far1, "n1": near1, "h1": home1, "f2": far2, "n2": near2, "fi": final,
    }
    for name, *where in ORDER:
        steps[name](*where)

    for copy in sends:
        copy.wait_send()
    for k in range(NC):

        @pl.when(jnp.logical_not(mine))
        def _():
            out_copy(k, 0).wait_send()
            if k >= DIRECT:
                for core in range(2):
                    on_copy(k, core).wait_send()


def fused(tiles, lam, sig, rows, mask, occ, b):
    sem = pltpu.SemaphoreType.DMA

    def vm(*shape):
        return pltpu.VMEM(shape, BF16)

    def twice(*shapes):
        return [sem(shape) for shape in shapes for _ in range(2)]

    hbm = pl.BlockSpec(memory_space=pl.ANY)
    vmem = pl.BlockSpec(memory_space=pltpu.VMEM)
    return pl.pallas_call(
        fused_kernel,
        out_shape=jax.ShapeDtypeStruct((BR, NW), BF16),
        in_specs=[hbm] * 7,
        out_specs=vmem,
        scratch_shapes=[
            vm(SLOTS, ROWS, BS, BS),
            pltpu.SMEM((4, SLOTS), jnp.int32),
            vm(2 * KW, NW),
            vm(NOCC, 96),
            vm(4, NOCC, BS),
            vm(4, 4, 2, 3, NOCC, BS),
            vm(SIG * NOCC, SLOTS * BS),
            pltpu.VMEM((SIG, NOCC * ROWS, BS), F32),
            vm(NC, 4, BR, KW),
            vm(NC, BR, KW),
            vm(NC, 2, BR, KW),
            vm(max(DIRECT, 1), 3, BR, KW),
            vm(NC, BR, KW),
            vm(NC, 2, 2, BR, KW),
            vm(NC, 2, 2, BR, HW),
            vm(2, 4, BR, HW),
            vm(2, 4, 2, BR, HW),
            vm(2, BR, HW),
            vm(2, 2, BR, HW),
            sem((8,)),
            sem((4,)),
            *twice((3,), (2, 3), (2, 4, 3), (2, 4, 4)),
            *twice((NC, 2), (NC, 2), (max(DIRECT, 1), 3)),
            sem((NC, 4)),
            sem((NC, 2, 4)),
            *twice((NC, 2), (2, 4, 2), (2, 4, 2, 2), (2, 2), (2, 2, 2)),
        ],
        compiler_params=pltpu.CompilerParams(
            collective_id=0, has_side_effects=True, vmem_limit_bytes=60 * 2**20
        ),
        name="fused",
    )(tiles, lam, sig, rows, mask, occ, b)


def body(integral_tiles, tile_lam, tile_sig, tile_rows, screen_mask, occ_panel, virt_panel):
    out = fused(
        integral_tiles, tile_lam, tile_sig, tile_rows, screen_mask, occ_panel, virt_panel
    )
    return out.reshape(2, ROWS, NW)


def solution(mesh):
    return jax.shard_map(
        body,
        mesh=mesh,
        in_specs=(
            P(("pair", "orb"), None, None, None),
            P(("pair", "orb")),
            P(("pair", "orb")),
            P(("pair", "orb")),
            P(("pair", "orb")),
            P(None, ("pair", "orb")),
            P("pair", "orb"),
        ),
        out_specs=P("pair", None, "orb"),
        check_vma=False,
    )
```

time: 88.2 us -> 87.4 us (level)
  Pallas kernels: 85.9 us -> 84.9 us
    pallas_call x1, Pallas kernels: 85.9 us -> 84.9 us  [fused(): pl.pallas_call(fused_kernel, out_shape=jax.ShapeDtypeStruct((BR, NW), BF1...]
where the time goes in v3:
time: 87.4 us; the launch traced here: 86.7 us
  Pallas kernels  84.9 us (97%)
  local copies, waits for them, and re-layouts  1.81 us (2%)
    pallas_call x1, Pallas kernels, fused(): pl.pallas_call(fused_kernel, out_shape=jax.ShapeDtypeStruct((BR, NW), BF1...  84.9 us
    unnamed x1, local copies, waits for them, and re-layouts  1.81 us

profile of v3, /device:TPU:1, one launch (start us, length us, event | category | flops | bytes accessed | tf_op | source)
XLA Modules:
  0.0 86.7 jit_solution(124060747113692192)
XLA Ops:
  0.0 84.9 %fused.1 = bf16[80,2816]{1,0:T(8,128)(2,1)} custom-call(bf16[12,40,128,128]{3,2,1,0:T(8,128)(2,1)} %tiles_hbm.1, s32[12]{0:T(128)} %lam_hbm.1, s32[12]{0:T(128)} %sig_hbm.1, s32[12]{0:T(128)} %rows_hbm.1, s32[12]{0:T(128)} %mask_hbm.1, bf16[64,96]{1,0:T(8,128)(2,1)} %occ_hbm.1, bf16[384,2816]{1,0:T(8,128)(2,1)} %b_hbm.1), custom_call_target="tpu_custom_call" | custom-call | tf_op jit(solution)/shard_map/fused/pallas_call | solution.py:453
  84.9 1.8 %copy.9 = bf16[2,40,2816]{2,1,0:T(8,128)(2,1)} copy(bf16[2,40,2816]{2,1,0:T(8,128)(2,1)} %bitcast.1) | data formatting | bytes 901120

commit v4 on v3

--- a/solution.py
+++ b/solution.py
@@ -193,7 +193,7 @@
                 keep, picked, jnp.zeros_like(picked)
             )
 
-    @pl.loop(0, ROWS // 2, unroll=4)
+    @pl.loop(0, ROWS // 2, unroll=10)
     def _(q):
         parts = []
         for t in range(SLOTS):
@@ -424,19 +424,23 @@
         "zf": z_far, "zn": z_near, "zs": z_sum, "zo": z_on, "mm": first_multiply,
         "f1": far1, "n1": near1, "h1": home1, "f2": far2, "n2": near2, "fi": final,
     }
+    def drain():
+        for copy in sends:
+            copy.wait_send()
+        for k in range(NC):
+
+            @pl.when(jnp.logical_not(mine))
+            def _():
+                out_copy(k, 0).wait_send()
+                if k >= DIRECT:
+                    for core in range(2):
+                        on_copy(k, core).wait_send()
+
     for name, *where in ORDER:
+        if name == "fi" and sends:
+            drain()
+            sends.clear()
         steps[name](*where)
-
-    for copy in sends:
-        copy.wait_send()
-    for k in range(NC):
-
-        @pl.when(jnp.logical_not(mine))
-        def _():
-            out_copy(k, 0).wait_send()
-            if k >= DIRECT:
-                for core in range(2):
-                    on_copy(k, core).wait_send()
 
 
 def fused(tiles, lam, sig, rows, mask, occ, b):

time: 87.4 us -> 86.6 us (level)
  Pallas kernels: 84.9 us -> 84 us
where the time goes in v4:
time: 86.6 us; the launch traced here: 85.9 us
  Pallas kernels  84 us (97%)
  local copies, waits for them, and re-layouts  1.81 us (2%)
    pallas_call x1, Pallas kernels, fused(): pl.pallas_call(fused_kernel, out_shape=jax.ShapeDtypeStruct((BR, NW), BF1...  84 us
    unnamed x1, local copies, waits for them, and re-layouts  1.81 us

profile of v4, /device:TPU:1, one launch (start us, length us, event | category | flops | bytes accessed | tf_op | source)
XLA Modules:
  0.0 85.9 jit_solution(13205858954547110644)
XLA Ops:
  0.0 84.0 %fused.1 = bf16[80,2816]{1,0:T(8,128)(2,1)} custom-call(bf16[12,40,128,128]{3,2,1,0:T(8,128)(2,1)} %tiles_hbm.1, s32[12]{0:T(128)} %lam_hbm.1, s32[12]{0:T(128)} %sig_hbm.1, s32[12]{0:T(128)} %rows_hbm.1, s32[12]{0:T(128)} %mask_hbm.1, bf16[64,96]{1,0:T(8,128)(2,1)} %occ_hbm.1, bf16[384,2816]{1,0:T(8,128)(2,1)} %b_hbm.1), custom_call_target="tpu_custom_call" | custom-call | tf_op jit(solution)/shard_map/fused/pallas_call | solution.py:457
  84.0 1.8 %copy.9 = bf16[2,40,2816]{2,1,0:T(8,128)(2,1)} copy(bf16[2,40,2816]{2,1,0:T(8,128)(2,1)} %bitcast.1) | data formatting | bytes 901120
